TPU v7x, 32 devices: a whole 2x2x4 slice. The times are simulated.
32 devices in a mesh: dp: 2 (over y), expert: 16 (over z, x, core).
Axes of the slice: x: 2, y: 2, z: 4, core: 2. Of those that a mesh axis runs over, the one named last changes fastest.
Arguments:
- tokens: bfloat16 [4096, 2048], P(('dp', 'expert')), may hold values from -6 to 6
- routes: int32 [4096, 2], P(('dp', 'expert')), may hold values from 0 to 15, all different within a row; in each aligned block of 128 rows (0 to 127, 128 to 255, ...) at most 24 rows name the same one
- gates: float32 [4096, 2], P(('dp', 'expert')), may hold values from 0.05 to 1
- grad_out: bfloat16 [4096, 2048], P(('dp', 'expert')), may hold values from -6 to 6
- w_gate: bfloat16 [16, 2048, 768], P('expert', 'dp'), may hold values from -0.125 to 0.125
- w_up: bfloat16 [16, 2048, 768], P('expert', 'dp'), may hold values from -0.125 to 0.125
- w_down: bfloat16 [16, 768, 2048], P('expert', None, 'dp'), may hold values from -0.21875 to 0.21875
Outputs:
- grad_tokens: bfloat16 [4096, 2048], P(('dp', 'expert'))
- grad_gates: float32 [4096, 2], P(('dp', 'expert'))
- grad_down: float32 [16, 768, 2048], P('expert', None, 'dp')
Inputs may be any that keep to these rules, and one draw needn't show every extreme that they name: Within the rows of one device no expert is named by more than 24 routes, a bound that some block reaches; the 2 experts of a token differ.
All inputs are finite; a program needn't handle non-finite values.
Results may differ from a plain program's by a relative error of at most 0.015.
Values may be sent and summed in bfloat16 or wider, within the bound.
No kernel may reach another device: no remote copies, remote signals or barrier semaphores. Data moves between devices by JAX's collectives and lax.ppermute only.
A program may use at most 128 MiB of HBM per device.

v0:
```python
import jax
import jax.numpy as jnp
from jax import lax
from jax.sharding import PartitionSpec as P


def silu_parts(pre):
    sig = jax.nn.sigmoid(pre)
    return (pre * sig, sig * (1.0 + pre * (1.0 - sig)))


def contract_last(left, right):
    return lax.dot_general(
        left, right, (((1,), (1,)), ((), ())), preferred_element_type=jnp.float32
    )


def contract_first(left, right):
    return lax.dot_general(
        left, right, (((0,), (0,)), ((), ())), preferred_element_type=jnp.float32
    )


def full_weights(w_gate, w_up, w_down):
    gathered = (
        lax.all_gather(w_gate, "dp", axis=1, tiled=True),
        lax.all_gather(w_up, "dp", axis=1, tiled=True),
    )
    down_full = lax.all_gather(w_down, "dp", axis=2, tiled=True)[0]
    return (gathered[0][0], gathered[1][0], down_full)


def expert_rows(x_rows, scaled, gate_full, up_full, down_full):
    pre_gate = jnp.dot(x_rows, gate_full, preferred_element_type=jnp.float32)
    pre_up = jnp.dot(x_rows, up_full, preferred_element_type=jnp.float32)
    act, slope = silu_parts(pre_gate)
    hidden_f = act * pre_up
    back = contract_last(scaled, down_full)
    score = jnp.sum(back * hidden_f, axis=1).astype(jnp.bfloat16)
    d_gate = (back * pre_up * slope).astype(jnp.bfloat16)
    d_up = (back * act).astype(jnp.bfloat16)
    route_grad = (contract_last(d_gate, gate_full) + contract_last(d_up, up_full)).astype(
        jnp.bfloat16
    )
    return (route_grad, score, hidden_f.astype(jnp.bfloat16))


def per_device(tokens, routes, gates, grad_out, w_gate, w_up, w_down):
    experts = lax.axis_size("expert")
    count = tokens.shape[0]
    width = tokens.shape[1]
    top = routes.shape[1]
    cap = 3 * count * top // (2 * experts)
    slots = experts * cap
    routed = count * top
    flat = routes.reshape(routed)
    labels = jnp.arange(experts, dtype=jnp.int32)
    onehot = (flat[:, None] == labels[None, :]).astype(jnp.int32)
    rank = jnp.sum((jnp.cumsum(onehot, axis=0) - onehot) * onehot, axis=1)
    position = flat * cap + rank
    owner = (
        jnp.full((slots,), routed, jnp.int32).at[position].set(jnp.arange(routed, dtype=jnp.int32))
    )
    source = owner // top
    padded_tokens = jnp.concatenate([tokens, jnp.zeros((1, width), tokens.dtype)], axis=0)
    padded_grads = jnp.concatenate([grad_out, jnp.zeros((1, width), grad_out.dtype)], axis=0)
    padded_gates = jnp.concatenate([gates.reshape(routed), jnp.zeros((1,), jnp.float32)], axis=0)
    inputs_out = padded_tokens[source].reshape(experts, cap, width)
    scaled_out = (padded_gates[owner][:, None] * padded_grads[source].astype(jnp.float32)).astype(
        jnp.bfloat16
    )
    scaled_out = scaled_out.reshape(experts, cap, width)
    arrived = (
        lax.all_to_all(inputs_out, "expert", split_axis=0, concat_axis=0, tiled=True),
        lax.all_to_all(scaled_out, "expert", split_axis=0, concat_axis=0, tiled=True),
    )
    x_rows = arrived[0].reshape(slots, width)
    scaled_rows = arrived[1].reshape(slots, width)
    gate_full, up_full, down_full = full_weights(w_gate, w_up, w_down)
    route_grad, score, hidden = expert_rows(x_rows, scaled_rows, gate_full, up_full, down_full)
    down_share = lax.psum_scatter(
        contract_first(scaled_rows, hidden).astype(jnp.bfloat16),
        "dp",
        scatter_dimension=0,
        tiled=True,
    ).astype(jnp.float32)
    grad_down = jnp.transpose(down_share)[None]
    returned = (
        lax.all_to_all(
            route_grad.reshape(experts, cap, width),
            "expert",
            split_axis=0,
            concat_axis=0,
            tiled=True,
        ),
        lax.all_to_all(
            score.reshape(experts, cap), "expert", split_axis=0, concat_axis=0, tiled=True
        ),
    )
    back_rows = returned[0].reshape(slots, width)
    back_scores = returned[1].reshape(slots)
    per_route = back_rows[position].reshape(count, top, width)
    grad_tokens = jnp.sum(per_route.astype(jnp.float32), axis=1).astype(jnp.bfloat16)
    grad_gates = back_scores[position].astype(jnp.float32).reshape(count, top) / gates
    return (grad_tokens, grad_gates, grad_down)


def solution(mesh):
    placed = (
        P(("dp", "expert"), None),
        P(("dp", "expert"), None),
        P(("dp", "expert"), None),
        P(("dp", "expert"), None),
        P("expert", "dp", None),
        P("expert", "dp", None),
        P("expert", None, "dp"),
    )
    return jax.shard_map(
        per_device,
        mesh=mesh,
        in_specs=placed,
        out_specs=(P(("dp", "expert"), None), P(("dp", "expert"), None), P("expert", None, "dp")),
        check_vma=False,
    )
```

profile of v0, /device:TPU:11, one launch (start us, length us, event | category | flops | bytes accessed | tf_op | source)
XLA Modules:
  0.0 226.1 jit_solution(777020998624058308)
XLA Ops:
  7.2 0.7 all-gather.8.cloned.1.call-update
  8.3 0.6 reduce-window.6
  9.6 1.4 scatter_custom_fusion
  11.0 3.1 %gather_fusion.2 = bf16[384,2048]{1,0:T(8,128)(2,1)} fusion(bf16[129,2048]{1,0:T(8,128)(2,1)S(1)} %concatenate.11, s32[1024]{0:T(1024)S(1)} %get-tuple-element.16), kind=kCustom, calls=%fused_computation.2 | custom fusion | bytes 3147264 | tf_op jit(solution)/shard_map/gather | solution.py:68
  14.1 6.6 %all-to-all-start.1 = ((bf16[16,24,2048]{2,1,0:T(8,128)(2,1)}), bf16[16,24,2048]{2,1,0:T(8,128)(2,1)}, u32[]{:S(2)}, u32[]{:S(2)}) async-start(bf16[16,24,2048]{2,1,0:T(8,128)(2,1)} %bitcast.6), calls=%async_computation.1 | async-start | bytes 3145728 | tf_op jit(solution)/shard_map/all_to_all | solution.py:74
  20.7 0.7 all-gather.6.cloned.1.call-update
  21.5 0.3 copy-done.1
  21.8 2.5 %gather_fusion.1 = bf16[384,2048]{1,0:T(8,128)(2,1)S(1)} fusion(bf16[129,2048]{1,0:T(8,128)(2,1)S(1)} %concatenate.10, s32[1024]{0:T(1024)S(1)} %get-tuple-element.16), kind=kCustom, calls=%fused_computation.1 | custom fusion | bytes 3147264 | tf_op jit(solution)/shard_map/gather | solution.py:69
  24.6 2.8 %gather_fusion = f32[384]{0:T(512)S(1)} fusion(f32[257]{0:T(512)S(1)} %pad_maximum_fusion, s32[1024]{0:T(1024)S(1)} %get-tuple-element.17), kind=kCustom, calls=%fused_computation | custom fusion | bytes 4608 | tf_op jit(solution)/shard_map/gather | solution.py:69
  27.5 1.5 fusion
  29.0 28.0 %all-to-all-done.1 = bf16[16,24,2048]{2,1,0:T(8,128)(2,1)} async-done(((bf16[16,24,2048]{2,1,0:T(8,128)(2,1)}), bf16[16,24,2048]{2,1,0:T(8,128)(2,1)}, u32[]{:S(2)}, u32[]{:S(2)}) %all-to-all-start.1) | async-done | bytes 1572896 | tf_op jit(solution)/shard_map/all_to_all | solution.py:74
  57.0 4.9 %all-to-all-start = ((bf16[16,24,2048]{2,1,0:T(8,128)(2,1)}), bf16[16,24,2048]{2,1,0:T(8,128)(2,1)S(1)}, u32[]{:S(2)}, u32[]{:S(2)}) async-start(bf16[16,24,2048]{2,1,0:T(8,128)(2,1)} %fusion), calls=%async_computation | async-start | bytes 3145728 | tf_op jit(solution)/shard_map/all_to_all | solution.py:75
  61.9 0.7 all-gather.4.cloned.1.call-update
  62.7 4.2 %fusion.3 = f32[384,768]{1,0:T(8,128)S(1)} fusion(bf16[384,2048]{1,0:T(8,128)(2,1)} %bitcast.7, bf16[1,2048,768]{2,1,0:T(8,128)(2,1)} %all-gather.8.cloned.1.call-done), kind=kOutput, calls=%fused_computation.11 | convolution fusion | flops 1207959552 | bytes 5898240 | tf_op jit(solution)/shard_map/dot_general | solution.py:34
  66.9 35.2 %all-gather.6.cloned.1.call-done = bf16[1,2048,768]{2,1,0:T(8,128)(2,1)} async-done(((bf16[1,1024,768]{2,1,0:T(8,128)(2,1)}), bf16[1,2048,768]{2,1,0:T(8,128)(2,1)}) %all-gather.6.cloned.1.call-update) | async-done | bytes 3145744 | tf_op jit(solution)/shard_map/all_gather | solution.py:27
  102.2 4.8 %fusion.7 = f32[384,768]{1,0:T(8,128)} fusion(bf16[384,2048]{1,0:T(8,128)(2,1)} %bitcast.7, bf16[1,2048,768]{2,1,0:T(8,128)(2,1)} %all-gather.6.cloned.1.call-done), kind=kOutput, calls=%fused_computation.15 | convolution fusion | flops 1207959552 | bytes 5898240 | tf_op jit(solution)/shard_map/dot_general | solution.py:35
  107.0 4.9 %convolution_convert_fusion = bf16[2048,768]{1,0:T(8,128)(2,1)} fusion(bf16[384,2048]{1,0:T(8,128)(2,1)S(1)} %bitcast.55, f32[384,768]{1,0:T(8,128)} %fusion.7, f32[384,768]{1,0:T(8,128)S(1)} %fusion.3), kind=kOutput, calls=%fused_computation.6 | convolution fusion | flops 1211301888 | bytes 7077888 | tf_op jit(solution)/shard_map/dot_general | solution.py:19
  112.0 36.7 %all-gather.4.cloned.1.call-done = bf16[1,768,2048]{2,1,0:T(8,128)(2,1)} async-done(((bf16[1,768,1024]{2,1,0:T(8,128)(2,1)}), bf16[1,768,2048]{2,1,0:T(8,128)(2,1)}) %all-gather.4.cloned.1.call-update) | async-done | bytes 3145744 | tf_op jit(solution)/shard_map/all_gather | solution.py:29
  148.7 4.8 %multiply_reduce_fusion = (bf16[384]{0:T(512)(128)(2,1)S(1)}, f32[384,768]{1,0:T(8,128)}) fusion(f32[384,768]{1,0:T(8,128)} %fusion.7, f32[384,768]{1,0:T(8,128)S(1)} %fusion.3, bf16[384,2048]{1,0:T(8,128)(2,1)S(1)} %bitcast.56, bf16[1,768,2048]{2,1,0:T(8,128)(2,1)} %all-gather.4.cloned.1.call-done), kind=kOutput, calls=%fused_computation.21 | convolution fusion | flops 1210023552 | bytes 8258304 | tf_op jit(solution)/shard_map/dot_general | solution.py:13
  153.5 0.7 convert_element_type.73
  154.2 6.4 %all-to-all-start.3 = ((bf16[16,1,24]{2,1,0:T(2,128)(2,1)}), bf16[16,1,24]{2,1,0:T(2,128)(2,1)S(1)}, u32[]{:S(2)}, u32[]{:S(2)}) async-start(bf16[16,1,24]{2,1,0:T(2,128)(2,1)} %convert_element_type.73), calls=%async_computation.3 | async-start | bytes 16384 | tf_op jit(solution)/shard_map/all_to_all | solution.py:96
  160.5 4.3 %fusion.1 = f32[384,2048]{1,0:T(8,128)S(1)} fusion(bf16[1,2048,768]{2,1,0:T(8,128)(2,1)} %all-gather.8.cloned.1.call-done, f32[384,768]{1,0:T(8,128)S(1)} %fusion.3, f32[384,768]{1,0:T(8,128)} %get-tuple-element.15, f32[384,768]{1,0:T(8,128)} %fusion.7), kind=kOutput, calls=%fused_computation.9 | convolution fusion | flops 1210908672 | bytes 9830400 | tf_op jit(solution)/shard_map/dot_general | solution.py:13
  164.9 2.6 %add_convert_fusion = bf16[384,2048]{1,0:T(8,128)(2,1)} fusion(f32[384,2048]{1,0:T(8,128)S(1)} %fusion.1, bf16[1,2048,768]{2,1,0:T(8,128)(2,1)S(1)} %copy-done.4, f32[384,768]{1,0:T(8,128)S(1)} %copy-done.5, f32[384,768]{1,0:T(8,128)S(1)} %fusion.3), kind=kOutput, calls=%fused_computation.20 | convolution fusion | flops 1211301888 | bytes 10223616 | tf_op jit(solution)/shard_map/dot_general | solution.py:13
  167.5 6.0 %all-to-all-start.2 = ((bf16[16,24,2048]{2,1,0:T(8,128)(2,1)}), bf16[16,24,2048]{2,1,0:T(8,128)(2,1)S(1)}, u32[]{:S(2)}, u32[]{:S(2)}) async-start(bf16[16,24,2048]{2,1,0:T(8,128)(2,1)} %bitcast.10), calls=%async_computation.2 | async-start | bytes 3145728 | tf_op jit(solution)/shard_map/all_to_all | solution.py:89
  173.7 1.9 gather_fusion.4
  175.8 0.6 copy.26
  176.5 33.3 %all-to-all-done.2 = bf16[16,24,2048]{2,1,0:T(8,128)(2,1)S(1)} async-done(((bf16[16,24,2048]{2,1,0:T(8,128)(2,1)}), bf16[16,24,2048]{2,1,0:T(8,128)(2,1)S(1)}, u32[]{:S(2)}, u32[]{:S(2)}) %all-to-all-start.2) | async-done | bytes 1572896 | tf_op jit(solution)/shard_map/all_to_all | solution.py:89
  209.7 1.4 gather_fusion.3
  211.1 0.7 reshape.113
  211.8 3.7 %reduce_sum.34 = bf16[128,2048]{1,0:T(8,128)(2,1)} reduce(bf16[128,2,2048]{2,1,0:T(2,128)(2,1)S(1)} %reshape.113, bf16[]{:T(256)} %constant.34.clone.1), dimensions={1}, to_apply=%region_4.5 | reduce | flops 262144 | bytes 1572866 | tf_op jit(solution)/shard_map/reduce_sum | solution.py:103
  215.6 1.6 convert_bitcast_fusion
  217.2 2.4 %copy.27 = f32[1,768,1024]{2,1,0:T(8,128)} copy(f32[1,768,1024]{1,2,0:T(8,128)S(1)} %convert_bitcast_fusion) | data formatting | bytes 6291456
  (46 shorter events, 1.9 us)
Async XLA Ops:
  7.2 0.8 copy-start.2
  7.2 2.2 copy-start
  7.2 55.5 %all-gather.8.cloned.1.call-start = ((), (), s32[]{:S(2)}) async-start(), calls=%async_computation.7 | async-start | bytes 4718592 | tf_op jit(solution)/shard_map/all_gather | solution.py:26
  14.1 42.8 %all-to-all-start.1 = ((bf16[16,24,2048]{2,1,0:T(8,128)(2,1)}), bf16[16,24,2048]{2,1,0:T(8,128)(2,1)}, u32[]{:S(2)}, u32[]{:S(2)}) async-start(bf16[16,24,2048]{2,1,0:T(8,128)(2,1)} %bitcast.6), calls=%async_computation.1 | async-start | bytes 3145728 | tf_op jit(solution)/shard_map/all_to_all | solution.py:74
  20.7 1.1 copy-start.1
  20.7 81.5 %all-gather.6.cloned.1.call-start = ((), (), s32[]{:S(2)}) async-start(), calls=%async_computation.6 | async-start | bytes 4718592 | tf_op jit(solution)/shard_map/all_gather | solution.py:27
  21.8 2.5 %copy-start.3 = (f32[128,2]{0,1:T(2,128)S(1)}, f32[128,2]{0,1:T(2,128)}, u32[]{:S(2)}) copy-start(f32[128,2]{0,1:T(2,128)} %param.9) | copy-start | bytes 3076
  57.0 50.0 %all-to-all-start = ((bf16[16,24,2048]{2,1,0:T(8,128)(2,1)}), bf16[16,24,2048]{2,1,0:T(8,128)(2,1)S(1)}, u32[]{:S(2)}, u32[]{:S(2)}) async-start(bf16[16,24,2048]{2,1,0:T(8,128)(2,1)} %fusion), calls=%async_computation | async-start | bytes 3145728 | tf_op jit(solution)/shard_map/all_to_all | solution.py:75
  61.9 86.8 %all-gather.4.cloned.1.call-start = ((), (), s32[]{:S(2)}) async-start(), calls=%async_computation.5 | async-start | bytes 4718592 | tf_op jit(solution)/shard_map/all_gather | solution.py:29
  62.6 152.9 %reduce-scatter.2.cloned.1.call-start = ((), (), s32[]{:S(2)}) async-start(), calls=%async_computation.8 | async-start | bytes 4718592 | tf_op jit(solution)/shard_map/reduce_scatter | solution.py:81
  154.2 13.4 %all-to-all-start.3 = ((bf16[16,1,24]{2,1,0:T(2,128)(2,1)}), bf16[16,1,24]{2,1,0:T(2,128)(2,1)S(1)}, u32[]{:S(2)}, u32[]{:S(2)}) async-start(bf16[16,1,24]{2,1,0:T(2,128)(2,1)} %convert_element_type.73), calls=%async_computation.3 | async-start | bytes 16384 | tf_op jit(solution)/shard_map/all_to_all | solution.py:96
  160.5 4.3 %copy-start.4 = (bf16[1,2048,768]{2,1,0:T(8,128)(2,1)S(1)}, bf16[1,2048,768]{2,1,0:T(8,128)(2,1)}, u32[]{:S(2)}) copy-start(bf16[1,2048,768]{2,1,0:T(8,128)(2,1)} %all-gather.6.cloned.1.call-done) | copy-start | bytes 9437188
  160.5 4.4 %copy-start.5 = (f32[384,768]{1,0:T(8,128)S(1)}, f32[384,768]{1,0:T(8,128)}, u32[]{:S(2)}) copy-start(f32[384,768]{1,0:T(8,128)} %get-tuple-element.15) | copy-start | bytes 3538948
  167.5 42.2 %all-to-all-start.2 = ((bf16[16,24,2048]{2,1,0:T(8,128)(2,1)}), bf16[16,24,2048]{2,1,0:T(8,128)(2,1)S(1)}, u32[]{:S(2)}, u32[]{:S(2)}) async-start(bf16[16,24,2048]{2,1,0:T(8,128)(2,1)} %bitcast.10), calls=%async_computation.2 | async-start | bytes 3145728 | tf_op jit(solution)/shard_map/all_to_all | solution.py:89
Sparse Core Ops, SparseCore 0:
  9.6 46.0 all-gather.7
  57.2 44.9 all-gather.5
  103.7 44.9 all-gather.3
  151.4 43.3 reduce-scatter.1
where the time goes:
time: 227 us; the launch traced here: 226 us
  waiting for transfers between devices  135 us (59%)
  matrix products  25.7 us (11%)
  starting transfers between devices  24 us (11%)
  local copies, waits for them, and re-layouts  19.3 us (9%)
  between operations  14 us (6%)
  other arithmetic  7.64 us (3%)
    all_gather x1, waiting for transfers between devices, full_weights(): down_full = lax.all_gather(w_down, 'dp', axis=2, tiled=True)[0]  36.7 us
    all_gather x1, waiting for transfers between devices, full_weights(): lax.all_gather(w_up, 'dp', axis=1, tiled=True)  35.2 us
    all_to_all x1, waiting for transfers between devices, per_device(): lax.all_to_all(route_grad.reshape(experts, cap, width), 'expert', split_a...  33.3 us
    all_to_all x1, waiting for transfers between devices, per_device(): lax.all_to_all(inputs_out, 'expert', split_axis=0, concat_axis=0, tiled=T...  28 us
    dot_general x3, matrix products, contract_last(): lax.dot_general(left, right, (((1,), (1,)), ((), ())), preferred_element_...  11.7 us
    all_to_all x1, starting transfers between devices, per_device(): lax.all_to_all(inputs_out, 'expert', split_axis=0, concat_axis=0, tiled=T...  6.55 us
    all_to_all x1, starting transfers between devices, per_device(): lax.all_to_all(score.reshape(experts, cap), 'expert', split_axis=0, conca...  6.37 us
    all_to_all x1, starting transfers between devices, per_device(): lax.all_to_all(route_grad.reshape(experts, cap, width), 'expert', split_a...  6.02 us
  transfers between devices with their start and end apart: 8, of which 4 were waited for; matrix products, arithmetic and copies ran while one was open for 21% of the time, Pallas kernels for 0%

commit v1 on v0

v1 whole, which is shorter than its diff:
```python
import functools

import jax
import jax.numpy as jnp
from jax import lax
from jax.experimental import pallas as pl
from jax.experimental.pallas import tpu as pltpu
from jax.sharding import PartitionSpec as P

LANES = 128
VMEM_BYTES = 56 * 1024 * 1024


def contract_last(left, right):
    return lax.dot_general(
        left, right, (((1,), (1,)), ((), ())), preferred_element_type=jnp.float32
    )


def contract_first(left, right):
    return lax.dot_general(
        left, right, (((0,), (0,)), ((), ())), preferred_element_type=jnp.float32
    )


def tile_of(extent, most):
    return most if extent % most == 0 else extent


def slot_positions(routes, experts, stride, base):
    top, count = routes.shape
    labels = lax.broadcasted_iota(jnp.int32, (experts, count), 0)
    named = [labels == routes[k : k + 1, :] for k in range(top)]
    marks = sum(jnp.where(m, 1.0, 0.0) for m in named)
    earlier = lax.broadcasted_iota(jnp.int32, (count, count), 0) < lax.broadcasted_iota(
        jnp.int32, (count, count), 1
    )
    rank = jnp.dot(
        marks.astype(jnp.bfloat16),
        jnp.where(earlier, 1.0, 0.0).astype(jnp.bfloat16),
        preferred_element_type=jnp.float32,
    )
    slot = rank + (labels * stride + base).astype(jnp.float32)
    return [
        jnp.sum(jnp.where(m, slot, 0.0), axis=0, keepdims=True).astype(jnp.int32) for m in named
    ]


def dispatch_tokens(experts, cap, group_ref, routes_ref, tokens_ref, out_ref, pos_ref, pick_ref):
    @pl.when(pl.program_id(0) == 0)
    def _():
        pos = slot_positions(routes_ref[...], experts, cap, 0)
        slots, count = pick_ref.shape
        rows = lax.broadcasted_iota(jnp.int32, (slots, count), 0)
        pick_ref[...] = sum(jnp.where(rows == p, 1.0, 0.0) for p in pos).astype(jnp.bfloat16)
        for k, p in enumerate(pos):
            pos_ref[k : k + 1, :] = p

    out_ref[...] = jnp.dot(
        pick_ref[...], tokens_ref[...], preferred_element_type=jnp.float32
    ).astype(out_ref.dtype)


def dispatch_scaled(experts, cap, groups, group_ref, meta_ref, own_ref, *rest):
    others, (out_ref, pick_ref, scale_ref) = rest[: groups - 1], rest[groups - 1 :]
    count = own_ref.shape[0]
    slots = out_ref.shape[0]

    @pl.when(pl.program_id(0) == 0)
    def _():
        rows = lax.broadcasted_iota(jnp.int32, (slots, count), 0)
        total = jnp.zeros((slots, 1), jnp.float32)
        for q in range(groups):
            top = meta_ref.shape[1] // 2
            routes = meta_ref[q, :top, :].astype(jnp.int32)
            pos = slot_positions(routes, experts, groups * cap, q * cap)
            hit = jnp.zeros((slots, count), jnp.float32)
            weight = jnp.zeros((slots, count), jnp.float32)
            for k, p in enumerate(pos):
                here = rows == p
                hit = hit + jnp.where(here, 1.0, 0.0)
                weight = weight + jnp.where(here, meta_ref[q, top + k : top + k + 1, :], 0.0)
            pick_ref[:, q * count : (q + 1) * count] = hit.astype(jnp.bfloat16)
            total = total + jnp.sum(weight, axis=1, keepdims=True)
        scale_ref[...] = jnp.broadcast_to(total, scale_ref.shape)

    grads = jnp.concatenate([own_ref[...]] + [ref[...] for ref in others], axis=0)
    rows = jnp.dot(pick_ref[...], grads, preferred_element_type=jnp.float32)
    out_ref[...] = (scale_ref[:, :1] * rows).astype(out_ref.dtype)


def expert_kernel(groups, x_ref, *refs):
    gates, ups = refs[:groups], refs[groups : 2 * groups]
    parts = refs[2 * groups : 3 * groups]
    back_out, hidden_out, d_gate_ref, d_up_ref, score_ref = refs[3 * groups :]
    rows = x_ref.shape[0]
    share, hidden = gates[0].shape
    step = tile_of(hidden, 256)
    score_ref[...] = jnp.zeros_like(score_ref)

    @pl.loop(0, hidden // step)
    def _(j):
        cols = pl.ds(pl.multiple_of(j * step, step), step)
        pre_gate = jnp.zeros((rows, step), jnp.float32)
        pre_up = jnp.zeros((rows, step), jnp.float32)
        back = jnp.zeros((rows, step), jnp.float32)
        for k in range(groups):
            x = x_ref[:, k * share : (k + 1) * share]
            pre_gate += jnp.dot(x, gates[k][:, cols], preferred_element_type=jnp.float32)
            pre_up += jnp.dot(x, ups[k][:, cols], preferred_element_type=jnp.float32)
            back += parts[k][:, cols].astype(jnp.float32)
        sig = jax.nn.sigmoid(pre_gate)
        act = pre_gate * sig
        slope = sig * (1.0 + pre_gate * (1.0 - sig))
        hidden_f = act * pre_up
        hidden_out[:, cols] = hidden_f.astype(jnp.bfloat16)
        score_ref[...] += jnp.sum(back * hidden_f, axis=1, keepdims=True)
        d_gate_ref[:, cols] = (back * pre_up * slope).astype(jnp.bfloat16)
        d_up_ref[:, cols] = (back * act).astype(jnp.bfloat16)

    width = groups * share
    back_out[:, width:] = jnp.broadcast_to(score_ref[:, :1], (rows, LANES)).astype(jnp.bfloat16)
    block = tile_of(share, 256)
    for k in range(groups):

        @pl.loop(0, share // block)
        def _(c):
            at = pl.ds(pl.multiple_of(c * block, block), block)
            grad = contract_last(d_gate_ref[...], gates[k][at, :])
            grad += contract_last(d_up_ref[...], ups[k][at, :])
            out = pl.ds(pl.multiple_of(k * share + c * block, block), block)
            back_out[:, out] = grad.astype(jnp.bfloat16)


def combine_kernel(group_ref, pos_ref, gate_ref, rows_ref, score_ref, tokens_ref, gates_ref):
    count, top = pos_ref.shape
    slots = rows_ref.shape[0]
    lanes = lax.broadcasted_iota(jnp.int32, (count, slots), 1)
    picks = [
        jnp.where(lanes == pos_ref[:, k : k + 1], 1.0, 0.0).astype(jnp.bfloat16)
        for k in range(top)
    ]
    tokens_ref[...] = jnp.dot(
        sum(picks), rows_ref[...], preferred_element_type=jnp.float32
    ).astype(tokens_ref.dtype)

    @pl.when(pl.program_id(0) == 0)
    def _():
        for k in range(top):
            score = jnp.dot(picks[k], score_ref[...], preferred_element_type=jnp.float32)
            gates_ref[:, k : k + 1] = score[:, :1] / gate_ref[:, k : k + 1]


def per_device(tokens, routes, gates, grad_out, w_gate, w_up, w_down):
    experts = lax.axis_size("expert")
    groups = lax.axis_size("dp")
    group = lax.axis_index("dp")
    count, width = tokens.shape
    top = routes.shape[1]
    cap = 3 * count * top // (2 * experts)
    slots = experts * cap
    share = width // groups
    hidden = w_gate.shape[2]
    params = pltpu.CompilerParams(vmem_limit_bytes=VMEM_BYTES)
    here = group.astype(jnp.int32).reshape(1)

    def shifted(value, by):
        return lax.ppermute(value, "dp", [(i, (i + by) % groups) for i in range(groups)])

    def own_block(k, here_ref):
        return lax.rem(here_ref[0] - k + groups, groups)

    routes_t = jnp.transpose(routes)
    meta = jnp.concatenate([routes_t.astype(jnp.float32), jnp.transpose(gates)], axis=0)
    metas = [meta] + [shifted(meta, k) for k in range(1, groups)]
    grads = [
        shifted(
            lax.dynamic_slice(grad_out, (0, lax.rem(group + k, groups) * share), (count, share)), k
        )
        for k in range(1, groups)
    ]
    gate_parts = [w_gate[0]] + [shifted(w_gate[0], k) for k in range(1, groups)]
    up_parts = [w_up[0]] + [shifted(w_up[0], k) for k in range(1, groups)]

    block = tile_of(share, 512)
    scaled = pl.pallas_call(
        functools.partial(dispatch_scaled, experts, cap, groups),
        out_shape=jax.ShapeDtypeStruct((groups * slots, share), jnp.bfloat16),
        grid_spec=pltpu.PrefetchScalarGridSpec(
            num_scalar_prefetch=1,
            grid=(share // block,),
            in_specs=[
                pl.BlockSpec((groups, 2 * top, count), lambda c, g: (0, 0, 0)),
                pl.BlockSpec((count, block), lambda c, g: (0, g[0] * (share // block) + c)),
            ]
            + [pl.BlockSpec((count, block), lambda c, g: (0, c))] * (groups - 1),
            out_specs=pl.BlockSpec((groups * slots, block), lambda c, g: (0, c)),
            scratch_shapes=[
                pltpu.VMEM((groups * slots, groups * count), jnp.bfloat16),
                pltpu.VMEM((groups * slots, LANES), jnp.float32),
            ],
        ),
        compiler_params=params,
        name="dispatch_scaled",
    )(here, jnp.stack(metas), grad_out, *grads)
    scaled_rows = lax.all_to_all(
        scaled.reshape(experts, groups * cap, share), "expert", split_axis=0, concat_axis=0, tiled=True
    ).reshape(groups * slots, share)

    sent, pos = pl.pallas_call(
        functools.partial(dispatch_tokens, experts, cap),
        out_shape=(
            jax.ShapeDtypeStruct((slots, width), jnp.bfloat16),
            jax.ShapeDtypeStruct((top, count), jnp.int32),
        ),
        grid_spec=pltpu.PrefetchScalarGridSpec(
            num_scalar_prefetch=1,
            grid=(groups,),
            in_specs=[
                pl.BlockSpec((top, count), lambda k, g: (0, 0)),
                pl.BlockSpec((count, share), lambda k, g: (0, own_block(k, g))),
            ],
            out_specs=(
                pl.BlockSpec((slots, share), lambda k, g: (0, k)),
                pl.BlockSpec((top, count), lambda k, g: (0, 0)),
            ),
            scratch_shapes=[pltpu.VMEM((slots, count), jnp.bfloat16)],
        ),
        compiler_params=params,
        name="dispatch_tokens",
    )(here, routes_t, tokens)
    x_rows = lax.all_to_all(
        sent.reshape(experts, cap, width), "expert", split_axis=0, concat_axis=0, tiled=True
    ).reshape(slots, width)

    partial = contract_last(scaled_rows, w_down[0]).reshape(experts, groups, cap, hidden)
    back_parts = [partial[:, 0].reshape(slots, hidden)] + [
        shifted(partial[:, k].reshape(slots, hidden).astype(jnp.bfloat16), -k)
        for k in range(1, groups)
    ]

    returning, hidden_own = pl.pallas_call(
        functools.partial(expert_kernel, groups),
        out_shape=(
            jax.ShapeDtypeStruct((slots, width + LANES), jnp.bfloat16),
            jax.ShapeDtypeStruct((slots, hidden), jnp.bfloat16),
        ),
        scratch_shapes=[
            pltpu.VMEM((slots, hidden), jnp.bfloat16),
            pltpu.VMEM((slots, hidden), jnp.bfloat16),
            pltpu.VMEM((slots, LANES), jnp.float32),
        ],
        compiler_params=params,
        name="expert_rows",
    )(x_rows, *gate_parts, *up_parts, *back_parts)

    returned = lax.all_to_all(
        returning.reshape(experts, cap, width + LANES),
        "expert",
        split_axis=0,
        concat_axis=0,
        tiled=True,
    ).reshape(slots, width + LANES)

    hiddens = [hidden_own] + [shifted(hidden_own, k) for k in range(1, groups)]
    hidden_all = jnp.stack([h.reshape(experts, cap, hidden) for h in hiddens], axis=1)
    grad_down = contract_first(hidden_all.reshape(groups * slots, hidden), scaled_rows)[None]

    grad_tokens, grad_gates = pl.pallas_call(
        combine_kernel,
        out_shape=(
            jax.ShapeDtypeStruct((count, width), jnp.bfloat16),
            jax.ShapeDtypeStruct((count, top), jnp.float32),
        ),
        grid_spec=pltpu.PrefetchScalarGridSpec(
            num_scalar_prefetch=1,
            grid=(groups,),
            in_specs=[
                pl.BlockSpec((count, top), lambda k, g: (0, 0)),
                pl.BlockSpec((count, top), lambda k, g: (0, 0)),
                pl.BlockSpec((slots, share), lambda k, g: (0, k)),
                pl.BlockSpec((slots, LANES), lambda k, g: (0, width // LANES)),
            ],
            out_specs=(
                pl.BlockSpec((count, share), lambda k, g: (0, own_block(k, g))),
                pl.BlockSpec((count, top), lambda k, g: (0, 0)),
            ),
        ),
        compiler_params=params,
        name="combine",
    )(here, jnp.transpose(pos), gates, returned, returned)
    return (grad_tokens, grad_gates, grad_down)


def solution(mesh):
    placed = (
        P(("dp", "expert"), None),
        P(("dp", "expert"), None),
        P(("dp", "expert"), None),
        P(("dp", "expert"), None),
        P("expert", "dp", None),
        P("expert", "dp", None),
        P("expert", None, "dp"),
    )
    return jax.shard_map(
        per_device,
        mesh=mesh,
        in_specs=placed,
        out_specs=(P(("dp", "expert"), None), P(("dp", "expert"), None), P("expert", None, "dp")),
        check_vma=False,
    )
```

time: 227 us -> 210 us (0.925)
  Pallas kernels: 0 us -> 21.5 us
  matrix products: 25.7 us -> 5.96 us
  between operations: 14 us -> 0.69 us
  local copies, waits for them, and re-layouts: 19.3 us -> 10.3 us
  waiting for transfers between devices: 135 us -> 142 us
  other arithmetic: 7.64 us -> 3.31 us
    ppermute x0 -> x6, waiting for transfers between devices: none -> 90 us  [shifted(): lax.ppermute(value, 'dp', [(i, (i + by) % groups) for i in range(groups)])]
    all_gather x3 -> x0, waiting for transfers between devices: 72 us -> none  [the longest x1 36.7 us: full_weights(): down_full = lax.all_gather(w_down, 'dp', axis=2, tiled=True)[0]]
    pallas_call x0 -> x4, Pallas kernels: none -> 21.5 us  [the longest x1 12.6 us: per_device(): pl.pallas_call(functools.partial(expert_kernel, groups), out_shape=(jax.S...]
    gather x5 -> x0, local copies, waits for them, and re-layouts: 11.7 us -> none  [the longest x1 3.11 us: per_device(): inputs_out = padded_tokens[source].reshape(experts, cap, width)]
    dot_general x2 -> x0, matrix products: 9.07 us -> none  [the longest x1 4.83 us: expert_rows(): pre_up = jnp.dot(x_rows, up_full, preferred_element_type=jnp.float32)]
    all_to_all x4 -> x3, waiting for transfers between devices: 61.3 us -> 52.4 us  [the longest x1 33.4 us: per_device(): lax.all_to_all(scaled.reshape(experts, groups * cap, share), 'expert', sp...]
    dot_general x3 -> x1, matrix products: 11.7 us -> 2.87 us  [contract_last(): lax.dot_general(left, right, (((1,), (1,)), ((), ())), preferred_element_...]
    ppermute x0 -> x6, starting transfers between devices: none -> 5.47 us  [shifted(): lax.ppermute(value, 'dp', [(i, (i + by) % groups) for i in range(groups)])]
  transfers between devices with their start and end apart: 8 -> 9, of which waited for: 4 -> 7; matrix products, arithmetic and copies ran while one was open for 21% -> 6% of each run, Pallas kernels for 0% -> 1%
where the time goes in v1:
time: 210 us; the launch traced here: 209 us
  waiting for transfers between devices  142 us (68%)
  starting transfers between devices  24.8 us (12%)
  Pallas kernels  21.5 us (10%)
  local copies, waits for them, and re-layouts  10.3 us (5%)
  matrix products  5.96 us (3%)
  other arithmetic  3.31 us (2%)
    ppermute x6, waiting for transfers between devices, shifted(): lax.ppermute(value, 'dp', [(i, (i + by) % groups) for i in range(groups)])  90 us
    all_to_all x1, waiting for transfers between devices, per_device(): lax.all_to_all(scaled.reshape(experts, groups * cap, share), 'expert', sp...  33.4 us
    all_to_all x1, waiting for transfers between devices, per_device(): lax.all_to_all(returning.reshape(experts, cap, width + LANES), 'expert',...  19 us
    pallas_call x1, Pallas kernels, per_device(): pl.pallas_call(functools.partial(expert_kernel, groups), out_shape=(jax.S...  12.6 us
    all_to_all x1, starting transfers between devices, per_device(): lax.all_to_all(scaled.reshape(experts, groups * cap, share), 'expert', sp...  7.43 us
    all_to_all x1, starting transfers between devices, per_device(): lax.all_to_all(returning.reshape(experts, cap, width + LANES), 'expert',...  6.98 us
    unnamed x20, local copies, waits for them, and re-layouts  6.51 us
    ppermute x6, starting transfers between devices, shifted(): lax.ppermute(value, 'dp', [(i, (i + by) % groups) for i in range(groups)])  5.47 us
  transfers between devices with their start and end apart: 9, of which 7 were waited for; matrix products, arithmetic and copies ran while one was open for 6% of the time, Pallas kernels for 1%

profile of v1, /device:TPU:11, one launch (start us, length us, event | category | flops | bytes accessed | tf_op | source)
XLA Modules:
  0.0 209.0 jit_solution(13525035784848150218)
XLA Ops:
  0.7 1.1 constant_dynamic-slice_fusion
  1.7 1.3 collective-permute-start.3
  3.7 0.7 fusion.2
  4.6 4.4 %collective-permute-done.2 = f32[4,128]{1,0:T(4,128)S(1)} collective-permute-done((f32[4,128]{1,0:T(4,128)S(1)}, f32[4,128]{1,0:T(4,128)S(1)}, u32[]{:S(2)}, u32[]{:S(2)}) %collective-permute-start.2) | collective-permute-done | bytes 2080 | tf_op jit(solution)/shard_map/ppermute | solution.py:168
  9.6 0.7 copy-done.6
  10.3 3.2 %dispatch_scaled.1 = bf16[768,1024]{1,0:T(8,128)(2,1)} custom-call(s32[1]{0:T(128)} %bitcast.group_ref, f32[2,4,128]{2,1,0:T(4,128)} %pad_maximum_fusion.1.meta_ref, bf16[128,2048]{1,0:T(8,128)(2,1)} %own_ref.1, bf16[128,1024]{1,0:T(8,128)(2,1)} %copy-done.6), custom_call_target="tpu_custom_call" | custom-call | tf_op jit(solution)/shard_map/dispatch_scaled/pallas_call | solution.py:186
  13.5 7.4 %all-to-all-start.1 = ((bf16[16,48,1024]{2,1,0:T(8,128)(2,1)}), bf16[16,48,1024]{2,1,0:T(8,128)(2,1)S(1)}, u32[]{:S(2)}, u32[]{:S(2)}) async-start(bf16[16,48,1024]{2,1,0:T(8,128)(2,1)} %bitcast.41), calls=%async_computation.1 | async-start | bytes 3145728 | tf_op jit(solution)/shard_map/all_to_all | solution.py:206
  20.9 2.8 %dispatch_tokens.1 = (bf16[384,2048]{1,0:T(8,128)(2,1)}, s32[2,128]{1,0:T(2,128)}) custom-call(s32[1]{0:T(128)} %bitcast.group_ref, s32[2,128]{1,0:T(2,128)} %bitcast.54, bf16[128,2048]{1,0:T(8,128)(2,1)} %tokens_ref.1), custom_call_target="tpu_custom_call" | custom-call | tf_op jit(solution)/shard_map/dispatch_tokens/pallas_call | solution.py:210
  23.7 33.4 %all-to-all-done.1 = bf16[16,48,1024]{2,1,0:T(8,128)(2,1)S(1)} async-done(((bf16[16,48,1024]{2,1,0:T(8,128)(2,1)}), bf16[16,48,1024]{2,1,0:T(8,128)(2,1)S(1)}, u32[]{:S(2)}, u32[]{:S(2)}) %all-to-all-start.1) | async-done | bytes 1572896 | tf_op jit(solution)/shard_map/all_to_all | solution.py:206
  57.1 1.1 copy-done.4
  58.3 4.9 %all-to-all-start = ((bf16[16,24,2048]{2,1,0:T(8,128)(2,1)}), bf16[16,24,2048]{2,1,0:T(8,128)(2,1)S(1)}, u32[]{:S(2)}, u32[]{:S(2)}) async-start(bf16[16,24,2048]{2,1,0:T(8,128)(2,1)} %bitcast.50), calls=%async_computation | async-start | bytes 3145728 | tf_op jit(solution)/shard_map/all_to_all | solution.py:232
  63.2 1.2 collective-permute-start
  64.6 2.9 %fusion = f32[16,2,24,768]{3,2,1,0:T(8,128)S(1)} fusion(bf16[16,2,24,1024]{3,2,1,0:T(8,128)(2,1)} %bitcast.48, bf16[1,768,1024]{2,1,0:T(8,128)(2,1)S(1)} %copy-done), kind=kOutput, calls=%fused_computation.1 | convolution fusion | flops 1207959552 | bytes 5505024 | tf_op jit(solution)/shard_map/dot_general | solution.py:15
  67.5 0.9 slice.12
  68.5 1.2 collective-permute-start.4
  69.7 1.1 slice.9
  70.8 28.2 %collective-permute-done.refs_1_ = bf16[1024,768]{1,0:T(8,128)(2,1)S(1)} collective-permute-done((bf16[1024,768]{1,0:T(8,128)(2,1)}, bf16[1024,768]{1,0:T(8,128)(2,1)S(1)}, u32[]{:S(2)}, u32[]{:S(2)}) %collective-permute-start) | collective-permute-done | bytes 1572896 | tf_op jit(solution)/shard_map/ppermute | solution.py:168
  99.0 1.2 copy-done.3
  100.2 32.6 %collective-permute-done.1.refs_3_ = bf16[1024,768]{1,0:T(8,128)(2,1)} collective-permute-done((bf16[1024,768]{1,0:T(8,128)(2,1)}, bf16[1024,768]{1,0:T(8,128)(2,1)}, u32[]{:S(2)}, u32[]{:S(2)}) %collective-permute-start.1) | collective-permute-done | bytes 1572896 | tf_op jit(solution)/shard_map/ppermute | solution.py:168
  132.8 12.6 %collective-permute-done.4.refs_5_ = bf16[384,768]{1,0:T(8,128)(2,1)} collective-permute-done((bf16[384,768]{1,0:T(8,128)(2,1)}, bf16[384,768]{1,0:T(8,128)(2,1)}, u32[]{:S(2)}, u32[]{:S(2)}) %collective-permute-start.4) | collective-permute-done | bytes 589856 | tf_op jit(solution)/shard_map/ppermute | solution.py:168
  145.5 12.6 %expert_rows.1 = (bf16[384,2176]{1,0:T(8,128)(2,1)}, bf16[384,768]{1,0:T(8,128)(2,1)}) custom-call(bf16[384,2048]{1,0:T(8,128)(2,1)} %bitcast.40, bf16[1024,768]{1,0:T(8,128)(2,1)} %bitcast.45, bf16[1024,768]{1,0:T(8,128)(2,1)} %copy-done.3, bf16[1024,768]{1,0:T(8,128)(2,1)} %bitcast.47, bf16[1024,768]{1,0:T(8,128)(2,1)} %collective-permute-done.1.refs_3_, ...), custom_call_target="tpu_custom_call" | custom-call | tf_op jit(solution)/shard_map/expert_rows/pallas_call | solution.py:242
  158.1 7.0 %all-to-all-start.2 = ((bf16[16,24,2176]{2,1,0:T(8,128)(2,1)}), bf16[16,24,2176]{2,1,0:T(8,128)(2,1)S(1)}, u32[]{:S(2)}, u32[]{:S(2)}) async-start(bf16[16,24,2176]{2,1,0:T(8,128)(2,1)} %bitcast.43), calls=%async_computation.2 | async-start | bytes 3342336 | tf_op jit(solution)/shard_map/all_to_all | solution.py:257
  165.1 1.2 collective-permute-start.5
  166.3 0.7 copy.14.gate_ref
  167.0 0.7 copy.13
  167.8 12.2 %collective-permute-done.5 = bf16[384,768]{1,0:T(8,128)(2,1)} collective-permute-done((bf16[384,768]{1,0:T(8,128)(2,1)}, bf16[384,768]{1,0:T(8,128)(2,1)}, u32[]{:S(2)}, u32[]{:S(2)}) %collective-permute-start.5) | collective-permute-done | bytes 589856 | tf_op jit(solution)/shard_map/ppermute | solution.py:168
  179.9 1.3 pad_maximum_fusion
  181.3 3.1 %convolution_bitcast_fusion = f32[1,768,1024]{2,1,0:T(8,128)} fusion(bf16[768,768]{1,0:T(8,128)(2,1)S(1)} %bitcast.51, bf16[768,1024]{1,0:T(8,128)(2,1)S(1)} %bitcast.49), kind=kOutput, calls=%fused_computation | convolution fusion | flops 1207959552 | bytes 5898240 | tf_op jit(solution)/shard_map/dot_general | solution.py:21
  184.4 19.0 %all-to-all-done.2 = bf16[16,24,2176]{2,1,0:T(8,128)(2,1)S(1)} async-done(((bf16[16,24,2176]{2,1,0:T(8,128)(2,1)}), bf16[16,24,2176]{2,1,0:T(8,128)(2,1)S(1)}, u32[]{:S(2)}, u32[]{:S(2)}) %all-to-all-start.2) | async-done | bytes 1671200 | tf_op jit(solution)/shard_map/all_to_all | solution.py:257
  203.3 1.2 copy-done.1
  204.6 2.9 %combine.1 = (bf16[128,2048]{1,0:T(8,128)(2,1)}, f32[128,2]{1,0:T(8,128)}) custom-call(s32[1]{0:T(128)} %bitcast.group_ref, s32[128,2]{1,0:T(8,128)} %bitcast.53, f32[128,2]{1,0:T(8,128)} %copy.14.gate_ref, bf16[384,2176]{1,0:T(8,128)(2,1)} %bitcast.38, bf16[384,2176]{1,0:T(8,128)(2,1)} %bitcast.39), custom_call_target="tpu_custom_call" | custom-call | tf_op jit(solution)/shard_map/combine/pallas_call | solution.py:269
  207.5 1.5 copy.17
  (20 shorter events, 1.8 us)
Async XLA Ops:
  0.6 64.0 %copy-start = (bf16[1,768,1024]{2,1,0:T(8,128)(2,1)S(1)}, bf16[1,768,1024]{2,1,0:T(8,128)(2,1)}, u32[]{:S(2)}) copy-start(bf16[1,768,1024]{2,1,0:T(8,128)(2,1)} %param.13) | copy-start | bytes 4718596
  1.7 7.9 %collective-permute-start.3 = (bf16[128,1024]{1,0:T(8,128)(2,1)S(1)}, bf16[128,1024]{1,0:T(8,128)(2,1)S(1)}, u32[]{:S(2)}, u32[]{:S(2)}) collective-permute-start(bf16[128,1024]{1,0:T(8,128)(2,1)S(1)} %constant_dynamic-slice_fusion), channel_id=1, source_target_pairs={{0,16},{16,0},{1,17},{17,1},{2,18},{18,2},{3,19},{19,3},{4,20},{20... | collective-permute-start | bytes 786440 | tf_op jit(solution)/shard_map/ppermute | solution.py:168
  4.4 4.6 %collective-permute-start.2 = (f32[4,128]{1,0:T(4,128)S(1)}, f32[4,128]{1,0:T(4,128)S(1)}, u32[]{:S(2)}, u32[]{:S(2)}) collective-permute-start(f32[4,128]{1,0:T(4,128)S(1)} %get-tuple-element.22), channel_id=1, source_target_pairs={{0,16},{16,0},{1,17},{17,1},{2,18},{18,2},{3,19},{19,3},{4,20},{20... | collective-permute-start | bytes 6152 | tf_op jit(solution)/shard_map/ppermute | solution.py:168
  9.6 0.7 copy-start.6
  13.5 43.6 %all-to-all-start.1 = ((bf16[16,48,1024]{2,1,0:T(8,128)(2,1)}), bf16[16,48,1024]{2,1,0:T(8,128)(2,1)S(1)}, u32[]{:S(2)}, u32[]{:S(2)}) async-start(bf16[16,48,1024]{2,1,0:T(8,128)(2,1)} %bitcast.41), calls=%async_computation.1 | async-start | bytes 3145728 | tf_op jit(solution)/shard_map/all_to_all | solution.py:206
  57.1 1.1 copy-start.4
  58.3 74.6 %all-to-all-start = ((bf16[16,24,2048]{2,1,0:T(8,128)(2,1)}), bf16[16,24,2048]{2,1,0:T(8,128)(2,1)S(1)}, u32[]{:S(2)}, u32[]{:S(2)}) async-start(bf16[16,24,2048]{2,1,0:T(8,128)(2,1)} %bitcast.50), calls=%async_computation | async-start | bytes 3145728 | tf_op jit(solution)/shard_map/all_to_all | solution.py:232
  63.2 35.8 %collective-permute-start = (bf16[1024,768]{1,0:T(8,128)(2,1)}, bf16[1024,768]{1,0:T(8,128)(2,1)S(1)}, u32[]{:S(2)}, u32[]{:S(2)}) collective-permute-start(bf16[1024,768]{1,0:T(8,128)(2,1)} %bitcast.44), channel_id=1, source_target_pairs={{0,16},{16,0},{1,17},{17,1},{2,18},{18,2},{3,19},{19,3},{4,20},{20... | collective-permute-start | bytes 4718600 | tf_op jit(solution)/shard_map/ppermute | solution.py:168
  64.4 68.4 %collective-permute-start.1 = (bf16[1024,768]{1,0:T(8,128)(2,1)}, bf16[1024,768]{1,0:T(8,128)(2,1)}, u32[]{:S(2)}, u32[]{:S(2)}) collective-permute-start(bf16[1024,768]{1,0:T(8,128)(2,1)} %bitcast.46), channel_id=1, source_target_pairs={{0,16},{16,0},{1,17},{17,1},{2,18},{18,2},{3,19},{19,3},{4,20},{20... | collective-permute-start | bytes 4718600 | tf_op jit(solution)/shard_map/ppermute | solution.py:168
  68.5 77.0 %collective-permute-start.4 = (bf16[384,768]{1,0:T(8,128)(2,1)}, bf16[384,768]{1,0:T(8,128)(2,1)}, u32[]{:S(2)}, u32[]{:S(2)}) collective-permute-start(bf16[384,768]{1,0:T(8,128)(2,1)} %bitcast.16), channel_id=1, source_target_pairs={{0,16},{16,0},{1,17},{17,1},{2,18},{18,2},{3,19},{19,3},{4,20},{20... | collective-permute-start | bytes 1769480 | tf_op jit(solution)/shard_map/ppermute | solution.py:168
  99.0 1.2 copy-start.3
  132.8 12.6 %copy-start.2 = (bf16[16,24,2048]{2,1,0:T(8,128)(2,1)}, bf16[16,24,2048]{2,1,0:T(8,128)(2,1)S(1)}, u32[]{:S(2)}) copy-start(bf16[16,24,2048]{2,1,0:T(8,128)(2,1)S(1)} %all-to-all-done) | copy-start | bytes 4718596
  158.1 8.2 %copy-start.7 = (f32[128,2]{0,1:T(2,128)S(1)}, f32[128,2]{0,1:T(2,128)}, u32[]{:S(2)}) copy-start(f32[128,2]{0,1:T(2,128)} %param.9) | copy-start | bytes 3076
  158.1 9.0 %copy-start.8 = (s32[2,128]{1,0:T(2,128)S(1)}, s32[2,128]{1,0:T(2,128)}, u32[]{:S(2)}) copy-start(s32[2,128]{1,0:T(2,128)} %get-tuple-element.9) | copy-start | bytes 3076
  158.1 45.3 %all-to-all-start.2 = ((bf16[16,24,2176]{2,1,0:T(8,128)(2,1)}), bf16[16,24,2176]{2,1,0:T(8,128)(2,1)S(1)}, u32[]{:S(2)}, u32[]{:S(2)}) async-start(bf16[16,24,2176]{2,1,0:T(8,128)(2,1)} %bitcast.43), calls=%async_computation.2 | async-start | bytes 3342336 | tf_op jit(solution)/shard_map/all_to_all | solution.py:257
  165.1 14.9 %collective-permute-start.5 = (bf16[384,768]{1,0:T(8,128)(2,1)}, bf16[384,768]{1,0:T(8,128)(2,1)}, u32[]{:S(2)}, u32[]{:S(2)}) collective-permute-start(bf16[384,768]{1,0:T(8,128)(2,1)} %get-tuple-element.14), channel_id=1, source_target_pairs={{0,16},{16,0},{1,17},{17,1},{2,18},{18,2},{3,19},{19,3},{4,20},{20... | collective-permute-start | bytes 1769480 | tf_op jit(solution)/shard_map/ppermute | solution.py:168
  167.8 13.5 %copy-start.5 = (bf16[16,48,1024]{2,1,0:T(8,128)(2,1)S(1)}, bf16[16,48,1024]{2,1,0:T(8,128)(2,1)}, u32[]{:S(2)}) copy-start(bf16[16,48,1024]{2,1,0:T(8,128)(2,1)} %copy-done.4) | copy-start | bytes 4718596
  203.3 1.2 copy-start.1
